TPU v7x, 768 devices: a whole 4x8x12 slice. The times are simulated.
768 devices in a mesh: prod: 12 (over z), store: 64 (over y, x, core).
Axes of the slice: x: 4, y: 8, z: 12, core: 2. Of those that a mesh axis runs over, the one named last changes fastest.
Arguments:
- tiles: bfloat16 [49152, 64, 512], P(('prod', 'store')), may hold values from -6 to 6
- tile_blocks: int32 [768, 64, 2], P(('prod', 'store')), may hold values from 0 to 63, as said below
- counts: int32 [768], P(('prod', 'store')), may hold values from 16 to 64, as said below
- fetch_list: int32 [768, 64, 1], P(('prod', 'store')), may hold values from 0 to 511, as said below
- store_factor: bfloat16 [32768, 128], P('store'), may hold values from -0.29882812 to 0.29882812
- day_factor: bfloat16 [8, 128], replicated, may hold values from -0.08984375 to 0.08984375
Outputs:
- product_factor: float32 [12288, 128], P(('prod', 'store'))
Inputs may be any that keep to these rules, and one draw needn't show every extreme that they name: `tile_blocks`: product block within the group (16) in column 0; in column 1 each device's slots name 64 different entries of its store list, a permutation. `counts`: one device in every draw has all 64 slots live. `fetch_list`: row o of a device's list holds 1 different store blocks owned by store index o, o * 8 to (o + 1) * 8 - 1.
All inputs are finite; a program needn't handle non-finite values.
Results may differ from a plain program's by a relative error of at most 0.007.
Values may be sent and summed in bfloat16 or wider, within the bound.
A program may use at most 32 MiB of HBM per device.

v0:
```python
import jax
import jax.numpy as jnp
from jax import lax
from jax.sharding import PartitionSpec as P

PB_DEV = 16
SB_DEV = 8


def group_terms(tile_vals, block_ids, count, start, table, day_factor):
    size = tile_vals.shape[0]
    rows = table[block_ids[:, 1]]
    kron = (
        rows.astype(jnp.float32)[:, :, None, :] * day_factor.astype(jnp.float32)[None, None, :, :]
    )
    kron = kron.reshape(size, -1, rows.shape[2]).astype(jnp.bfloat16)
    contrib = jnp.einsum("tij,tjr->tir", tile_vals, kron, preferred_element_type=jnp.float32)
    live = (start + jnp.arange(size, dtype=jnp.int32) < count).astype(jnp.float32)
    onehot = (block_ids[:, 0][:, None] == jnp.arange(PB_DEV, dtype=jnp.int32)[None, :]).astype(
        jnp.float32
    ) * live[:, None]
    return jnp.einsum("tp,tir->pir", onehot, contrib, preferred_element_type=jnp.float32)


def local(tiles, tile_blocks, counts, fetch_list, store_factor, day_factor):
    nprod = lax.axis_size("prod")
    tile_size = tiles.shape[1]
    store_size = store_factor.shape[0] // SB_DEV
    rank_size = store_factor.shape[1]
    row_ids = jnp.arange(store_factor.shape[0], dtype=jnp.int32)
    chosen = row_ids % nprod == lax.axis_index("prod")
    masked = jnp.where(chosen[:, None], store_factor, jnp.zeros_like(store_factor))
    gram_part = lax.dot_general(
        masked, store_factor, (((0,), (0,)), ((), ())), preferred_element_type=jnp.float32
    )
    gram_store = lax.psum(gram_part, ("prod", "store"))
    wanted = fetch_list[0]
    whole = lax.all_gather(store_factor, "store", axis=0, tiled=True)
    table = whole.reshape(-1, store_size, rank_size)[wanted.reshape(-1)]
    count = counts[0]
    group = 8

    def add_group(index, total):
        start = index * group
        tile_vals = lax.dynamic_slice_in_dim(tiles, start, group, 0)
        block_ids = lax.dynamic_slice_in_dim(tile_blocks[0], start, group, 0)
        return total + group_terms(tile_vals, block_ids, count, start, table, day_factor)

    empty = jnp.zeros((PB_DEV, tile_size, rank_size), jnp.float32)
    total = lax.fori_loop(0, tiles.shape[0] // group, add_group, empty)
    share = lax.psum_scatter(total.reshape(-1, rank_size), "store", scatter_dimension=0, tiled=True)
    gram_day = jnp.dot(day_factor.T, day_factor, preferred_element_type=jnp.float32)
    lower = jnp.linalg.cholesky(gram_store * gram_day)
    return jax.scipy.linalg.cho_solve((lower, True), share.T).T


def solution(mesh):
    return jax.shard_map(
        local,
        mesh=mesh,
        in_specs=(
            P(("prod", "store"), None, None),
            P(("prod", "store"), None, None),
            P(("prod", "store")),
            P(("prod", "store"), None, None),
            P("store", None),
            P(),
        ),
        out_specs=P(("prod", "store"), None),
        check_vma=False,
    )
```

profile of v0, /device:TPU:1, one launch (start us, length us, event | category | flops | bytes accessed | tf_op | source)
XLA Modules:
  0.0 731.0 jit_solution(17389137069940446104)
XLA Ops:
  7.4 1.9 fusion.15
  10.0 1.3 dynamic-slice.3
  12.7 458.8 %all-reduce.4.cloned.1.call-done = f32[128,128]{0,1:T(8,128)} async-done(((f32[128,128]{0,1:T(8,128)}), f32[128,128]{0,1:T(8,128)}) %all-reduce.4.cloned.1.call-update) | async-done | bytes 65552 | tf_op jit(solution)/shard_map/psum | solution.py:36
  471.5 1.1 convolution_multiply_fusion
  472.7 11.7 %cholesky.16 = f32[128,128]{1,0:T(8,128)S(1)} custom-call(f32[128,128]{1,0:T(8,128)S(1)} %fusion.23), custom_call_target="Cholesky" | custom-call | tf_op jit(solution)/shard_map/jit(cholesky)/cholesky | solution.py:53
  484.5 4.1 gather_fusion.1
  488.6 36.4 %while.14 = (s32[]{:T(128)}, f32[16,64,128]{2,0,1:T(8,128)S(1)}, s32[1,64,2]{1,2,0:T(2,128)}, s32[]{:T(128)}, bf16[64,64,512]{2,1,0:T(8,128)(2,1)}, /*index=5*/b...) while((s32[]{:T(128)}, f32[16,64,128]{2,0,1:T(8,128)S(1)}, ...), condition=%wide.region_4.5_spmd.clone, body=%wide.region_3.4_spmd.clone.sunk | while | flops 70584632 | bytes 3291709 | solution.py:50
  489.3 0.8 dynamic-slice_bitcast_fusion.2
  491.4 1.4 fusion.46
  493.8 0.8 dynamic-slice_bitcast_fusion.2
  495.9 1.4 fusion.46
  498.4 0.8 dynamic-slice_bitcast_fusion.2
  500.5 1.4 fusion.46
  502.9 0.8 dynamic-slice_bitcast_fusion.2
  505.0 1.4 fusion.46
  509.6 1.4 fusion.46
  514.1 1.4 fusion.46
  518.7 1.4 fusion.46
  523.2 1.4 fusion.46
  525.0 1.0 copy.18
  527.3 9.8 %custom-call.10 = f32[1,128,128]{1,2,0:T(8,128)S(1)} custom-call(f32[1,128,128]{2,1,0:T(8,128)S(1)} %fusion.18), custom_call_target="InvertDiagBlocksLowerTriangular" | custom-call | tf_op jit(solution)/shard_map/jit(_cho_solve)/triangular_solve | solution.py:54
  537.1 184.8 %all-reduce.6.cloned.1.call-done = f32[1024,128]{1,0:T(8,128)} async-done(((f32[1024,128]{1,0:T(8,128)}), f32[1024,128]{1,0:T(8,128)}) %all-reduce.6.cloned.1.call-update) | async-done | bytes 524304
  721.9 0.9 fusion.21
  722.8 0.8 fusion.19
  (84 shorter events, 24.6 us)
Async XLA Ops:
  7.4 464.1 %all-reduce.4.cloned.1.call-start = ((), (), s32[]{:S(2)}) async-start(), calls=%async_computation | async-start | bytes 131072 | tf_op jit(solution)/shard_map/psum | solution.py:36
  9.3 475.2 %all-gather.2.cloned.1.call-start = ((), (), s32[]{:S(2)}) async-start(), calls=%async_computation.1 | async-start | bytes 8519680 | tf_op jit(solution)/shard_map/all_gather | solution.py:38
  9.9 712.0 %all-reduce.6.cloned.1.call-start = ((), (), s32[]{:S(2)}) async-start(), calls=%async_computation.2 | async-start | bytes 1048576
Sparse Core Ops, SparseCore 0:
  13.6 457.8 all-reduce.3
Sparse Core Ops, SparseCore 1:
  14.4 102.2 all-gather.1
  526.1 195.8 all-reduce.5
where the time goes:
time: 733 us; the launch traced here: 731 us
  waiting for transfers between devices  644 us (88%)
  other arithmetic  34.5 us (5%)
  matrix products  18.8 us (3%)
  local copies, waits for them, and re-layouts  17.3 us (2%)
  between operations  15.6 us (2%)
    psum x1, waiting for transfers between devices, local(): gram_store = lax.psum(gram_part, ('prod', 'store'))  459 us
    unnamed x4, waiting for transfers between devices  185 us
  transfers between devices with their start and end apart: 3, of which 2 were waited for; matrix products, arithmetic and copies ran while one was open for 4% of the time, Pallas kernels for 0%

commit v1 on v0

v1 whole, which is shorter than its diff:
```python
import jax
import jax.numpy as jnp
from jax import lax
from jax.experimental import pallas as pl
from jax.experimental.pallas import tpu as pltpu
from jax.sharding import PartitionSpec as P

PB = 16
SB = 8
TS = 64
RANK = 128
DAYS = 8
X = 8
Y = 8
HIGHEST = lax.Precision.HIGHEST
F32 = jnp.float32


def rows_sum(x):
    return jnp.sum(x, axis=0, keepdims=True)


def cols_sum(x):
    return jnp.sum(x, axis=1, keepdims=True)


def plan(blocks, count):
    slots = blocks.shape[1]
    sub = lax.broadcasted_iota(jnp.int32, (slots, slots), 0)
    lane = lax.broadcasted_iota(jnp.int32, (slots, slots), 1)
    lane_row = lax.broadcasted_iota(jnp.int32, (1, slots), 1)
    p_row, perm_row = blocks[0:1, :], blocks[1:2, :]
    key_row = jnp.where(lane_row < count, p_row * slots, PB * slots * 4) + perm_row
    eye = sub == lane
    perm_col = cols_sum(jnp.where(eye, perm_row, 0))
    key_col = cols_sum(jnp.where(eye, key_row, 0))
    rank_col = cols_sum(jnp.where(key_row < key_col, 1, 0))
    tile_of = rows_sum(jnp.where(perm_col == lane, sub, 0))
    order = rows_sum(jnp.where(rank_col == lane, perm_col, 0))
    block_at = rows_sum(jnp.where(rank_col == lane, key_col // slots, 0))
    block_before = rows_sum(jnp.where(rank_col + 1 == lane, key_col // slots, 0))
    same = jnp.where((block_at == block_before) & (lane_row > 0), 1, 0)
    ends = rows_sum(jnp.where(key_col < (lane + 1) * slots, 1, 0))
    begins = rows_sum(jnp.where(key_col < lane * slots, 1, 0))
    return tile_of, order, same, ends, begins


def kernel(
    tiles_hbm, blocks_ref, count_ref, fetch_ref, store_hbm, day_ref, out_ref,
    tiles, own, right1, right2, right3, left1, left2, left3, far,
    table, stage, contribs, sums,
    plan_v, plan_s, my_list, lists_v, lists_s,
    gram_part, gram_y, gram_mine, gram_x, gram_sum, gram, inverse,
    send_x, recv_x, send_y, recv_y,
    local_sem, ring_s, ring_r, list_s, list_r, block_s, block_r,
    gy_s, gy_r, gx_s, gx_r, gg_s, gg_r, rx_s, rx_r, ry_s, ry_r,
):
    me = lax.axis_index("store")
    y, q = me // X, me % X

    def x_peer(d):
        return y * X + (q + d) % X

    def y_peer(e):
        return (y + e) % Y * X + q

    def to(src, dst, send, recv, target):
        return pltpu.make_async_remote_copy(
            src_ref=src, dst_ref=dst, send_sem=send, recv_sem=recv,
            device_id={"store": target}, device_id_type=pl.DeviceIdType.MESH,
        )

    def each(first, last, body):
        def step(i, carry):
            body(i)
            return carry
        lax.fori_loop(first, last, step, 0)

    load_own = pltpu.make_async_copy(store_hbm, own, local_sem.at[0])
    load_own.start()
    load_tiles = pltpu.make_async_copy(tiles_hbm, tiles, local_sem.at[1])
    load_tiles.start()
    barrier = pltpu.get_barrier_semaphore()
    each(1, X, lambda d: pl.semaphore_signal(
        barrier, inc=1, device_id={"store": x_peer(d)}, device_id_type=pl.DeviceIdType.MESH))
    each(1, Y, lambda e: pl.semaphore_signal(
        barrier, inc=1, device_id={"store": y_peer(e)}, device_id_type=pl.DeviceIdType.MESH))

    for row, value in enumerate(plan(blocks_ref[...], count_ref[0])):
        plan_v[row : row + 1, 0:64] = value
    my_list[0:1, 0:64] = fetch_ref[...]
    load_plan = pltpu.make_async_copy(plan_v, plan_s, local_sem.at[2])
    load_plan.start()
    load_own.wait()
    gram_part[...] = lax.dot_general(
        own[...].reshape(SB * TS, RANK), own[...].reshape(SB * TS, RANK),
        (((0,), (0,)), ((), ())), preferred_element_type=F32,
    )
    load_plan.wait()
    pl.semaphore_wait(barrier, X + Y - 2)

    rights, lefts = [right1, right2, right3, far], [left1, left2, left3, far]
    half = SB // 2

    def ring(direction, step, part):
        bufs = rights if direction == 0 else lefts
        src = own if step == 0 else bufs[step - 1]
        cut = pl.ds(part * half, half)
        return to(
            src.at[cut], bufs[step].at[cut],
            ring_s.at[direction, step, part], ring_r.at[direction, step, part],
            y_peer(1 if direction == 0 else Y - 1),
        )

    for part in range(2):
        ring(0, 0, part).start()
        ring(1, 0, part).start()

    def list_copy(d):
        return to(my_list, lists_v.at[d], list_s.at[d], list_r.at[d], x_peer(d))

    each(1, X, lambda d: list_copy(d).start())

    def gram_y_copy(e):
        return to(
            gram_part.at[pl.ds((y + e) % Y * 16, 16)], gram_y.at[y],
            gy_s.at[e], gy_r.at[e], y_peer(e),
        )

    each(1, Y, lambda e: gram_y_copy(e).start())
    gram_y[y] = gram_part[pl.ds(y * 16, 16), :]

    lists_v[0] = my_list[...]
    each(1, X, lambda d: list_copy(d).wait_recv())
    load_lists = pltpu.make_async_copy(lists_v, lists_s, local_sem.at[3])
    load_lists.start()
    load_lists.wait()

    def block_copy(k, d):
        return to(stage.at[k, d], table.at[k, d], block_s.at[k, d], block_r.at[k, d], x_peer(d))

    def owner(k, d):
        shift = (0, Y - 1, 1, Y - 2, 2, Y - 3, 3, 4)[k]
        return (y + shift) % Y * X + (q + X - d) % X

    def serve(k, buf):
        mine = owner(k, 0)
        table[k, 0] = buf[lists_s[0, 0, mine] & (SB - 1)]

        def one(d):
            stage[k, d] = buf[lists_s[X - d, 0, mine] & (SB - 1)]
            block_copy(k, d).start()

        each(1, X, one)

    day = day_ref[...].astype(F32)

    def contribute(k):
        def one(d):
            entry = owner(k, d)
            rows = table[k, d].astype(F32)
            kron = (rows[:, None, :] * day[None, :, :]).reshape(TS * DAYS, RANK).astype(jnp.bfloat16)
            contribs[entry] = jnp.dot(
                tiles[plan_s[0, entry] & 63], kron, preferred_element_type=F32
            )

        each(1, X, lambda d: block_copy(k, d).wait_recv())
        each(0, X, one)

    def forward(step):
        for part in range(2):
            for direction in range(2):
                ring(direction, step - 1, part).wait_recv()
                if step < 3 or part == direction:
                    ring(direction, step, part).start()

    lane8 = lax.broadcasted_iota(jnp.int32, (8, RANK), 1)
    sub8 = lax.broadcasted_iota(jnp.int32, (8, RANK), 0)
    lane_all = lax.broadcasted_iota(jnp.int32, (RANK, RANK), 1)

    def eliminate(b):
        first = b * 8
        old = inverse[pl.ds(pl.multiple_of(first, 8), 8), :]
        panel = old
        for r in range(8):
            at = lane8 == first + r
            column = cols_sum(jnp.where(at, panel, 0.0))
            panel = jnp.where(at, jnp.where(sub8 == r, 1.0, 0.0), panel)
            pivot = panel[r : r + 1, :] / column[r : r + 1, :]
            panel = jnp.where(sub8 == r, pivot, panel - column * pivot)
        done = lane8 < first
        within = (lane8 >= first) & (lane8 < first + 8)
        left = jnp.where(within, 0.0, jnp.where(done, -old, old))
        change = lax.dot_general(
            left, panel, (((0,), (0,)), ((), ())), precision=HIGHEST, preferred_element_type=F32
        )
        inside = (lane_all >= first) & (lane_all < first + 8)
        inverse[...] = jnp.where(inside, 0.0, inverse[...]) - change
        inverse[pl.ds(pl.multiple_of(first, 8), 8), :] = panel

    serve(0, own)
    forward(1)
    serve(1, right1)
    serve(2, left1)

    each(1, Y, lambda e: gram_y_copy(e).wait_recv())
    total = gram_y[0]
    for i in range(1, Y):
        total = total + gram_y[i]
    gram_mine[...] = total

    def gram_x_copy(d):
        return to(gram_mine, gram_x.at[q], gx_s.at[d], gx_r.at[d], x_peer(d))

    each(1, X, lambda d: gram_x_copy(d).start())
    gram_x[q] = total
    load_tiles.wait()
    contribute(0)

    forward(2)
    serve(3, right2)
    serve(4, left2)

    each(1, X, lambda d: gram_x_copy(d).wait_recv())
    total = gram_x[0]
    for i in range(1, X):
        total = total + gram_x[i]
    gram_sum[...] = total

    def gram_g_copy(e):
        return to(gram_sum, gram.at[y], gg_s.at[e], gg_r.at[e], y_peer(e))

    each(1, Y, lambda e: gram_g_copy(e).start())
    gram[y] = total
    contribute(1)

    forward(3)
    serve(5, right3)
    serve(6, left3)
    contribute(2)

    each(1, Y, lambda e: gram_g_copy(e).wait_recv())
    gram_day = lax.dot_general(
        day_ref[...], day_ref[...], (((0,), (0,)), ((), ())), preferred_element_type=F32
    )
    inverse[...] = gram[...].reshape(RANK, RANK) * gram_day

    ring(0, 3, 0).wait_recv()
    ring(1, 3, 1).wait_recv()
    serve(7, far)
    contribute(3)
    contribute(4)
    each(0, 8, eliminate)
    contribute(5)
    contribute(6)
    contribute(7)

    def add(r, run):
        run = contribs[plan_s[1, r] & 63] + jnp.where(plan_s[2, r] == 1, run, 0.0)
        sums[r] = run
        return run

    lax.fori_loop(0, 64, add, jnp.zeros((TS, RANK), F32))

    def pick(i):
        for j in range(2):
            p = 2 * i + j
            end = plan_s[3, p]
            value = sums[jnp.maximum(end - 1, 0) & 63]
            value = jnp.where(end > plan_s[4, p], value, 0.0).astype(jnp.bfloat16)
            for part in range(4):
                send_x[4 * j + part, i] = value[16 * part : 16 * part + 16]

    each(0, 8, pick)

    def rx_copy(d):
        return to(send_x.at[(q + d) % X], recv_x.at[d], rx_s.at[d], rx_r.at[d], x_peer(d))

    each(1, X, lambda d: rx_copy(d).start())
    each(8, 12, eliminate)
    each(1, X, lambda d: rx_copy(d).wait_recv())
    share = send_x[q].astype(F32)
    for d in range(1, X):
        share = share + recv_x[d].astype(F32)
    send_y[...] = share.astype(jnp.bfloat16)

    def ry_copy(e):
        return to(send_y.at[(y + e) % Y], recv_y.at[e], ry_s.at[e], ry_r.at[e], y_peer(e))

    each(1, Y, lambda e: ry_copy(e).start())
    each(12, 16, eliminate)
    each(1, Y, lambda e: ry_copy(e).wait_recv())
    mine = send_y[y].astype(F32)
    for e in range(1, Y):
        mine = mine + recv_y[e].astype(F32)
    out_ref[...] = jnp.dot(mine, inverse[...], precision=HIGHEST, preferred_element_type=F32)

    for direction in range(2):
        for step in range(4):
            for part in range(2):
                if step < 3 or part == direction:
                    ring(direction, step, part).wait_send()
    for k in range(8):
        each(1, X, lambda d: block_copy(k, d).wait_send())

    def sent(d):
        list_copy(d).wait_send()
        gram_y_copy(d).wait_send()
        gram_x_copy(d).wait_send()
        gram_g_copy(d).wait_send()
        rx_copy(d).wait_send()
        ry_copy(d).wait_send()

    each(1, 8, sent)


def local(tiles, tile_blocks, counts, fetch_list, store_factor, day_factor):
    blocks = tile_blocks[0].T
    fetch = fetch_list.reshape(1, -1)
    store = store_factor.reshape(SB, TS, RANK)
    vmem = pl.BlockSpec(memory_space=pltpu.VMEM)
    hbm = pl.BlockSpec(memory_space=pl.ANY)
    bf16 = jnp.bfloat16
    dma = pltpu.SemaphoreType.DMA
    ring_buf = pltpu.VMEM((SB, TS, RANK), bf16)
    return pl.pallas_call(
        kernel,
        out_shape=jax.ShapeDtypeStruct((16, RANK), F32),
        in_specs=[hbm, vmem, pl.BlockSpec(memory_space=pltpu.SMEM), vmem, hbm, vmem],
        out_specs=vmem,
        scratch_shapes=[
            pltpu.VMEM(tiles.shape, bf16),
            ring_buf, ring_buf, ring_buf, ring_buf, ring_buf, ring_buf, ring_buf, ring_buf,
            pltpu.VMEM((Y, X, TS, RANK), bf16),
            pltpu.VMEM((Y, X, TS, RANK), bf16),
            pltpu.VMEM((X * Y, 64, RANK), F32),
            pltpu.VMEM((64, 64, RANK), F32),
            pltpu.VMEM((8, 128), jnp.int32),
            pltpu.SMEM((8, 128), jnp.int32),
            pltpu.VMEM((8, 128), jnp.int32),
            pltpu.VMEM((X, 8, 128), jnp.int32),
            pltpu.SMEM((X, 8, 128), jnp.int32),
            pltpu.VMEM((RANK, RANK), F32),
            pltpu.VMEM((Y, 16, RANK), F32),
            pltpu.VMEM((16, RANK), F32),
            pltpu.VMEM((X, 16, RANK), F32),
            pltpu.VMEM((16, RANK), F32),
            pltpu.VMEM((Y, 16, RANK), F32),
            pltpu.VMEM((RANK, RANK), F32),
            pltpu.VMEM((X, Y, 16, RANK), bf16),
            pltpu.VMEM((X, Y, 16, RANK), bf16),
            pltpu.VMEM((Y, 16, RANK), bf16),
            pltpu.VMEM((Y, 16, RANK), bf16),
            dma((4,)),
            dma((2, 4, 2)), dma((2, 4, 2)),
            dma((8,)), dma((8,)),
            dma((8, 8)), dma((8, 8)),
            dma((8,)), dma((8,)), dma((8,)), dma((8,)), dma((8,)), dma((8,)),
            dma((8,)), dma((8,)), dma((8,)), dma((8,)),
        ],
        compiler_params=pltpu.CompilerParams(
            collective_id=0, has_side_effects=True, vmem_limit_bytes=60 * 1024 * 1024
        ),
    )(tiles, blocks, counts, fetch, store, day_factor)


def solution(mesh):
    return jax.shard_map(
        local,
        mesh=mesh,
        in_specs=(
            P(("prod", "store"), None, None),
            P(("prod", "store"), None, None),
            P(("prod", "store")),
            P(("prod", "store"), None, None),
            P("store", None),
            P(),
        ),
        out_specs=P(("prod", "store"), None),
        check_vma=False,
    )
```

time: 733 us -> 62.4 us (0.09)
  waiting for transfers between devices: 644 us -> 0 us
  Pallas kernels: 0 us -> 60.3 us
  other arithmetic: 34.5 us -> 0 us
  matrix products: 18.8 us -> 0 us
  local copies, waits for them, and re-layouts: 17.3 us -> 1.3 us
  between operations: 15.6 us -> 0.66 us
    psum x1 -> x0, waiting for transfers between devices: 459 us -> none  [local(): gram_store = lax.psum(gram_part, ('prod', 'store'))]
    unnamed x4 -> x0, waiting for transfers between devices: 185 us -> none
    pallas_call x0 -> x1, Pallas kernels: none -> 60.3 us  [local(): pl.pallas_call(kernel, out_shape=jax.ShapeDtypeStruct((16, RANK), F32), i...]
    another operation x5 -> x0, other arithmetic: 22.8 us -> none  [the longest x3 12.4 us: local(): lower = jnp.linalg.cholesky(gram_store * gram_day)]
    dot_general x18 -> x0, matrix products: 17.1 us -> none  [the longest x8 10.9 us: group_terms(): jnp.einsum('tij,tjr->tir', tile_vals, kron, preferred_element_type=jnp.fl...]
    convert_element_type x24 -> x0, other arithmetic: 10.8 us -> none  [the longest x8 5.47 us: group_terms(): day_factor.astype(jnp.float32)[None, None, :, :]]
    gather x9 -> x0, local copies, waits for them, and re-layouts: 8.69 us -> none  [the longest x8 4.56 us: group_terms(): rows = table[block_ids[:, 1]]]
  transfers between devices with their start and end apart: 3 -> 0, of which waited for: 2 -> 0; matrix products, arithmetic and copies ran while one was open for 4% -> 0% of each run, Pallas kernels for 0% -> 0%
where the time goes in v1:
time: 62.4 us; the launch traced here: 62.2 us
  Pallas kernels  60.3 us (97%)
  local copies, waits for them, and re-layouts  1.3 us (2%)
  between operations  0.66 us (1%)
    pallas_call x1, Pallas kernels, local(): pl.pallas_call(kernel, out_shape=jax.ShapeDtypeStruct((16, RANK), F32), i...  60.3 us
    unnamed x1, local copies, waits for them, and re-layouts  1.3 us

profile of v1, /device:TPU:1, one launch (start us, length us, event | category | flops | bytes accessed | tf_op | source)
XLA Modules:
  0.0 62.2 jit_solution(9448930130650010087)
XLA Ops:
  0.7 60.3 %shard_map.64 = f32[16,128]{1,0:T(8,128)} custom-call(bf16[64,64,512]{2,1,0:T(8,128)(2,1)} %tiles_hbm.1, s32[2,64]{1,0:T(2,128)} %bitcast.6, s32[1]{0:T(128)S(6)} %copy.8.count_ref, s32[1,64]{1,0:T(1,128)} %bitcast.7, bf16[8,64,128]{2,1,0:T(8,128)(2,1)} %bitcast.5, bf16[8,128]{1,0:T(8,128)(2,1)} %day_ref.1), custom_call_target="tpu_custom_call" | custom-call | tf_op jit(solution)/shard_map/pallas_call | solution.py:326
  60.9 1.3 %copy.9 = f32[16,128]{1,0:T(8,128)} copy(f32[16,128]{1,0:T(8,128)} %shard_map.64) | data formatting | bytes 16384

commit v2 on v1

v2 whole, which is shorter than its diff:
```python
import jax
import jax.numpy as jnp
from jax import lax
from jax.experimental import pallas as pl
from jax.experimental.pallas import tpu as pltpu
from jax.sharding import PartitionSpec as P

PB = 16
SB = 8
TS = 64
RANK = 128
DAYS = 8
X = 8
Y = 8
HIGHEST = lax.Precision.HIGHEST
F32 = jnp.float32


def rows_sum(x):
    return jnp.sum(x, axis=0, keepdims=True)


def cols_sum(x):
    return jnp.sum(x, axis=1, keepdims=True)


def plan(blocks, count):
    slots = blocks.shape[1]
    sub = lax.broadcasted_iota(jnp.int32, (slots, slots), 0)
    lane = lax.broadcasted_iota(jnp.int32, (slots, slots), 1)
    lane_row = lax.broadcasted_iota(jnp.int32, (1, slots), 1)
    p_row, perm_row = blocks[0:1, :], blocks[1:2, :]
    key_row = jnp.where(lane_row < count, p_row * slots, PB * slots * 4) + perm_row
    eye = sub == lane
    perm_col = cols_sum(jnp.where(eye, perm_row, 0))
    key_col = cols_sum(jnp.where(eye, key_row, 0))
    rank_col = cols_sum(jnp.where(key_row < key_col, 1, 0))
    tile_of = rows_sum(jnp.where(perm_col == lane, sub, 0))
    order = rows_sum(jnp.where(rank_col == lane, perm_col, 0))
    block_at = rows_sum(jnp.where(rank_col == lane, key_col // slots, 0))
    block_before = rows_sum(jnp.where(rank_col + 1 == lane, key_col // slots, 0))
    same = jnp.where((block_at == block_before) & (lane_row > 0), 1, 0)
    ends = rows_sum(jnp.where(key_col < (lane + 1) * slots, 1, 0))
    begins = rows_sum(jnp.where(key_col < lane * slots, 1, 0))
    return tile_of, order, same, ends, begins


def kernel(
    tiles_hbm, blocks_hbm, count_ref, fetch_hbm, store_hbm, day_hbm, out_ref,
    blocks_ref, fetch_ref, day_ref, tiles, own, right1, right2, right3, left1, left2, left3, far,
    table, stage, contribs, sums,
    plan_v, plan_s, my_list, lists_v, lists_s,
    gram_part, gram_x, gram_sum, gram, inverse,
    send_x, recv_x, send_y, recv_y,
    local_sem, ring_s, ring_r, list_s, list_r, block_s, block_r,
    gx_s, gx_r, gg_s, gg_r, rx_s, rx_r, ry_s, ry_r,
):
    me = lax.axis_index("store")
    y, q = me // X, me % X

    def x_peer(d):
        return y * X + (q + d) % X

    def y_peer(e):
        return (y + e) % Y * X + q

    def to(src, dst, send, recv, target):
        return pltpu.make_async_remote_copy(
            src_ref=src, dst_ref=dst, send_sem=send, recv_sem=recv,
            device_id={"store": target}, device_id_type=pl.DeviceIdType.MESH,
        )

    def each(first, last, body, unroll=1):
        def step(i, carry):
            body(i)
            return carry
        lax.fori_loop(first, last, step, 0, unroll=unroll)

    barrier = pltpu.get_barrier_semaphore()

    def greet(target):
        pl.semaphore_signal(
            barrier, inc=1, device_id={"store": target}, device_id_type=pl.DeviceIdType.MESH)

    def load(src, dst, i):
        copy = pltpu.make_async_copy(src, dst, local_sem.at[i])
        copy.start()
        return copy

    greet(y_peer(1))
    greet(y_peer(Y - 1))
    each(1, X, lambda d: greet(x_peer(d)))
    load_fetch = load(fetch_hbm, fetch_ref, 0)
    load_own = load(store_hbm, own, 1)
    load_blocks = load(blocks_hbm, blocks_ref, 2)
    load_day = load(day_hbm, day_ref, 3)
    load_tiles = load(tiles_hbm, tiles, 4)
    load_fetch.wait()
    my_list[0:1, 0:64] = fetch_ref[...]
    load_own.wait()
    pl.semaphore_wait(barrier, X + 1)

    def list_copy(d):
        return to(
            my_list.at[0:1], lists_v.at[d, 0:1], list_s.at[d], list_r.at[d], x_peer(d)
        )

    each(1, X, lambda d: list_copy(d).start())

    rights, lefts = [right1, right2, right3, far], [left1, left2, left3, far]
    parts, size = 4, SB // 4

    def ring(direction, step, part):
        bufs = rights if direction == 0 else lefts
        src = own if step == 0 else bufs[step - 1]
        cut = pl.ds(part * size, size)
        return to(
            src.at[cut], bufs[step].at[cut],
            ring_s.at[direction, step, part], ring_r.at[direction, step, part],
            y_peer(1 if direction == 0 else Y - 1),
        )

    for part in range(parts):
        ring(0, 0, part).start()
        ring(1, 0, part).start()

    def gram_add(*bufs):
        total = None
        for buf in bufs:
            rows = buf[...].reshape(SB * TS, RANK)
            part = lax.dot_general(
                rows, rows, (((0,), (0,)), ((), ())), preferred_element_type=F32
            )
            total = part if total is None else total + part
        return total

    load_blocks.wait()
    for row, value in enumerate(plan(blocks_ref[...], count_ref[0])):
        plan_v[row : row + 1, 0:64] = value
    load_plan = load(plan_v, plan_s, 5)
    lists_v[0, 0:1] = my_list[0:1]


    def block_copy(k, d):
        return to(stage.at[k, d], table.at[k, d], block_s.at[k, d], block_r.at[k, d], x_peer(d))

    def owner(k, d):
        shift = (0, Y - 1, 1, Y - 2, 2, Y - 3, 3, 4)[k]
        return (y + shift) % Y * X + (q + X - d) % X

    def serve(k, buf):
        mine = owner(k, 0)
        table[k, 0] = buf[lists_s[0, 0, mine] & (SB - 1)]

        def one(d):
            stage[k, d] = buf[lists_s[X - d, 0, mine] & (SB - 1)]
            block_copy(k, d).start()

        each(1, X, one)

    load_day.wait()
    day = day_ref[...].astype(F32)

    def contribute(k):
        def one(d):
            entry = owner(k, d)
            rows = table[k, d].astype(F32)
            kron = (rows[:, None, :] * day[None, :, :]).reshape(TS * DAYS, RANK).astype(jnp.bfloat16)
            contribs[entry] = jnp.dot(
                tiles[plan_s[0, entry] & 63], kron, preferred_element_type=F32
            )

        each(1, X, lambda d: block_copy(k, d).wait_recv())
        each(0, X, one, unroll=4)

    def forward(step):
        for part in range(parts):
            for direction in range(2):
                ring(direction, step - 1, part).wait_recv()
                if step < 3 or part // 2 == direction:
                    ring(direction, step, part).start()

    lane8 = lax.broadcasted_iota(jnp.int32, (8, RANK), 1)
    sub8 = lax.broadcasted_iota(jnp.int32, (8, RANK), 0)
    lane_all = lax.broadcasted_iota(jnp.int32, (RANK, RANK), 1)
    sub_all = lax.broadcasted_iota(jnp.int32, (RANK, RANK), 0)

    def lane_of(rows, at):
        return jnp.broadcast_to(cols_sum(jnp.where(lane8 == at, rows, 0.0)), (8, RANK))

    def sub_of(rows, r):
        return jnp.broadcast_to(rows[r : r + 1, :], (8, RANK))

    def invert8(rows, first):
        columns = [lane_of(rows, first + r) for r in range(8)]
        d = {(i, j): sub_of(columns[j], i) for j in range(8) for i in range(j + 1)}
        for k in range(8):
            recip = 1.0 / d[k, k]
            row = [d[min(i, k), max(i, k)] for i in range(8)]
            scaled = [x * recip for x in row]
            for j in range(8):
                for i in range(j + 1):
                    if i != k and j != k:
                        d[i, j] = d[i, j] - scaled[i] * row[j]
            for i in range(8):
                if i != k:
                    d[min(i, k), max(i, k)] = scaled[i]
            d[k, k] = -recip
        out = []
        for r in range(8):
            column = -d[r, 7]
            for i in range(7):
                column = jnp.where(sub8 == i, -d[min(i, r), max(i, r)], column)
            out.append(column)
        return out

    def gj_apply(left, done_rows, first):
        change = lax.dot_general(
            left, done_rows, (((0,), (0,)), ((), ())), precision=HIGHEST, preferred_element_type=F32
        )
        inside = (lane_all >= first) & (lane_all < first + 8)
        rows_in = (sub_all >= first) & (sub_all < first + 8)
        new = jnp.where(inside, 0.0, inverse[...]) - change
        inverse[...] = jnp.where(rows_in, jnp.broadcast_to(done_rows[None], (16, 8, RANK)).reshape(RANK, RANK), new)

    def gj_start():
        zero = jnp.zeros((8, RANK), F32)
        return inverse[0:8, :], zero, zero

    def gj_step(b, state):
        rows, left, done_rows = state
        first = b * 8
        gj_apply(left, done_rows, first - 8)
        within = (lane8 >= first) & (lane8 < first + 8)
        columns = invert8(rows, first)
        unit = jnp.where(within, jnp.where(lane8 - first == sub8, 1.0, 0.0), rows)
        new = columns[0] * sub_of(unit, 0)
        for r in range(1, 8):
            new = new + columns[r] * sub_of(unit, r)
        new_left = jnp.where(within, 0.0, jnp.where(lane8 < first, -rows, rows))
        after = inverse[pl.ds(pl.multiple_of(jnp.minimum(first + 8, RANK - 8), 8), 8), :]
        step = lane_of(after, first) * sub_of(new, 0)
        for r in range(1, 8):
            step = step + lane_of(after, first + r) * sub_of(new, r)
        return jnp.where(within, 0.0, after) - step, new_left, new

    def gj_end(state):
        gj_apply(state[1], state[2], RANK - 8)

    gram_part[...] = gram_add(own)
    forward(1)
    each(1, X, lambda d: list_copy(d).wait_recv())
    load(lists_v, lists_s, 6).wait()
    serve(0, own)
    serve(1, right1)
    serve(2, left1)
    gram_part[...] += gram_add(right1, left1)
    forward(2)
    serve(3, right2)
    serve(4, left2)
    gram_part[...] += gram_add(right2, left2)
    forward(3)
    serve(5, right3)
    serve(6, left3)
    gram_part[...] += gram_add(right3, left3)
    for part in range(2):
        ring(0, 3, part).wait_recv()
        ring(1, 3, 2 + part).wait_recv()
    serve(7, far)
    gram_part[...] += gram_add(far)

    gram_x[q] = gram_part[pl.ds(y * 16, 16), :]

    def gram_x_copy(d):
        return to(
            gram_part.at[pl.ds(y * 16, 16)], gram_x.at[q], gx_s.at[d], gx_r.at[d], x_peer(d)
        )

    def gram_g_copy(e):
        return to(gram_sum, gram.at[y], gg_s.at[e], gg_r.at[e], y_peer(e))

    each(1, X, lambda d: gram_x_copy(d).start())
    load_tiles.wait()
    load_plan.wait()
    for k in range(5):
        contribute(k)
    each(1, X, lambda d: gram_x_copy(d).wait_recv())
    total = gram_x[0]
    for i in range(1, X):
        total = total + gram_x[i]
    gram_sum[...] = total
    gram[y] = total
    each(1, Y, lambda e: gram_g_copy(e).start())
    contribute(5)
    contribute(6)
    contribute(7)

    def add(r, run):
        run = contribs[plan_s[1, r] & 63] + jnp.where(plan_s[2, r] == 1, run, 0.0)
        sums[r] = run
        return run

    lax.fori_loop(0, 64, add, jnp.zeros((TS, RANK), F32), unroll=8)

    def pick(i):
        place = (i + Y - y + 5) % Y
        for j in range(2):
            p = 2 * i + j
            end = plan_s[3, p]
            value = sums[jnp.maximum(end - 1, 0) & 63]
            value = jnp.where(end > plan_s[4, p], value, 0.0).astype(jnp.bfloat16)
            for part in range(4):
                send_x[4 * j + part, place] = value[16 * part : 16 * part + 16]

    each(0, 8, pick, unroll=2)

    cuts = (pl.ds(0, 3), pl.ds(3, 5))

    def rx_copy(d, part):
        return to(
            send_x.at[(q + d) % X, cuts[part]], recv_x.at[d, cuts[part]],
            rx_s.at[part, d], rx_r.at[part, d], x_peer(d),
        )

    def ry_copy(e):
        return to(send_y.at[(e + 5) % Y], recv_y.at[e], ry_s.at[e], ry_r.at[e], y_peer(e))

    def sum_x(part):
        each(1, X, lambda d: rx_copy(d, part).wait_recv())
        share = send_x[q, cuts[part]].astype(F32)
        for d in range(1, X):
            share = share + recv_x[d, cuts[part]].astype(F32)
        send_y[cuts[part]] = share.astype(jnp.bfloat16)

    for part in range(2):
        each(1, X, lambda d: rx_copy(d, part).start())
    each(1, Y, lambda e: gram_g_copy(e).wait_recv())
    gram_day = lax.dot_general(
        day_ref[...], day_ref[...], (((0,), (0,)), ((), ())), preferred_element_type=F32
    )
    inverse[...] = gram[...].reshape(RANK, RANK) * gram_day
    state = lax.fori_loop(0, 8, gj_step, gj_start())
    sum_x(0)
    each(3, 6, lambda e: ry_copy(e).start())
    state = lax.fori_loop(8, 10, gj_step, state)
    sum_x(1)
    each(1, 3, lambda e: ry_copy(e).start())
    each(6, 8, lambda e: ry_copy(e).start())
    gj_end(lax.fori_loop(10, 16, gj_step, state))

    for direction in range(2):
        for step in range(4):
            for part in range(parts):
                if step < 3 or part // 2 == direction:
                    ring(direction, step, part).wait_send()
    for k in range(8):
        each(1, X, lambda d: block_copy(k, d).wait_send())

    def sent(d):
        list_copy(d).wait_send()
        gram_x_copy(d).wait_send()
        gram_g_copy(d).wait_send()
        rx_copy(d, 0).wait_send()
        rx_copy(d, 1).wait_send()

    each(1, 8, sent)

    each(1, Y, lambda e: ry_copy(e).wait_recv())
    mine = send_y[5].astype(F32)
    for e in range(1, Y):
        mine = mine + recv_y[e].astype(F32)
    each(1, Y, lambda e: ry_copy(e).wait_send())
    out_ref[...] = jnp.dot(mine, inverse[...], precision=HIGHEST, preferred_element_type=F32)


def local(tiles, tile_blocks, counts, fetch_list, store_factor, day_factor):
    blocks = tile_blocks[0].T
    fetch = fetch_list.reshape(1, -1)
    store = store_factor.reshape(SB, TS, RANK)
    vmem = pl.BlockSpec(memory_space=pltpu.VMEM)
    hbm = pl.BlockSpec(memory_space=pl.ANY)
    bf16 = jnp.bfloat16
    dma = pltpu.SemaphoreType.DMA
    ring_buf = pltpu.VMEM((SB, TS, RANK), bf16)
    return pl.pallas_call(
        kernel,
        out_shape=jax.ShapeDtypeStruct((16, RANK), F32),
        in_specs=[hbm, hbm, pl.BlockSpec(memory_space=pltpu.SMEM), hbm, hbm, hbm],
        out_specs=vmem,
        scratch_shapes=[
            pltpu.VMEM(blocks.shape, jnp.int32), pltpu.VMEM(fetch.shape, jnp.int32), pltpu.VMEM(day_factor.shape, bf16),
            pltpu.VMEM(tiles.shape, bf16),
            ring_buf, ring_buf, ring_buf, ring_buf, ring_buf, ring_buf, ring_buf, ring_buf,
            pltpu.VMEM((Y, X, TS, RANK), bf16),
            pltpu.VMEM((Y, X, TS, RANK), bf16),
            pltpu.VMEM((X * Y, 64, RANK), F32),
            pltpu.VMEM((64, 64, RANK), F32),
            pltpu.VMEM((8, 128), jnp.int32),
            pltpu.SMEM((8, 128), jnp.int32),
            pltpu.VMEM((8, 128), jnp.int32),
            pltpu.VMEM((X, 8, 128), jnp.int32),
            pltpu.SMEM((X, 8, 128), jnp.int32),
            pltpu.VMEM((RANK, RANK), F32),
            pltpu.VMEM((X, 16, RANK), F32),
            pltpu.VMEM((16, RANK), F32),
            pltpu.VMEM((Y, 16, RANK), F32),
            pltpu.VMEM((RANK, RANK), F32),
            pltpu.VMEM((X, Y, 16, RANK), bf16),
            pltpu.VMEM((X, Y, 16, RANK), bf16),
            pltpu.VMEM((Y, 16, RANK), bf16),
            pltpu.VMEM((Y, 16, RANK), bf16),
            dma((8,)),
            dma((2, 4, 4)), dma((2, 4, 4)),
            dma((8,)), dma((8,)),
            dma((8, 8)), dma((8, 8)),
            dma((8,)), dma((8,)), dma((8,)), dma((8,)),
            dma((2, 8)), dma((2, 8)), dma((8,)), dma((8,)),
        ],
        compiler_params=pltpu.CompilerParams(
            collective_id=0, has_side_effects=True, vmem_limit_bytes=60 * 1024 * 1024
        ),
    )(tiles, blocks, counts, fetch, store, day_factor)


def solution(mesh):
    return jax.shard_map(
        local,
        mesh=mesh,
        in_specs=(
            P(("prod", "store"), None, None),
            P(("prod", "store"), None, None),
            P(("prod", "store")),
            P(("prod", "store"), None, None),
            P("store", None),
            P(),
        ),
        out_specs=P(("prod", "store"), None),
        check_vma=False,
    )
```

time: 62.4 us -> 49.2 us (0.79)
  Pallas kernels: 60.3 us -> 47.1 us
    pallas_call x1, Pallas kernels: 60.3 us -> 47.1 us  [local(): pl.pallas_call(kernel, out_shape=jax.ShapeDtypeStruct((16, RANK), F32), i...]
where the time goes in v2:
time: 49.2 us; the launch traced here: 49 us
  Pallas kernels  47.1 us (96%)
  local copies, waits for them, and re-layouts  1.3 us (3%)
  between operations  0.66 us (1%)
    pallas_call x1, Pallas kernels, local(): pl.pallas_call(kernel, out_shape=jax.ShapeDtypeStruct((16, RANK), F32), i...  47.1 us
    unnamed x1, local copies, waits for them, and re-layouts  1.3 us

profile of v2, /device:TPU:1, one launch (start us, length us, event | category | flops | bytes accessed | tf_op | source)
XLA Modules:
  0.0 49.0 jit_solution(6821103648247309360)
XLA Ops:
  0.7 47.1 %shard_map.64 = f32[16,128]{1,0:T(8,128)} custom-call(bf16[64,64,512]{2,1,0:T(8,128)(2,1)} %tiles_hbm.1, s32[2,64]{1,0:T(2,128)} %bitcast.6, s32[1]{0:T(128)S(6)} %copy.8.count_ref, s32[1,64]{1,0:T(1,128)} %bitcast.7, bf16[8,64,128]{2,1,0:T(8,128)(2,1)} %bitcast.5, bf16[8,128]{1,0:T(8,128)(2,1)} %day_hbm.1), custom_call_target="tpu_custom_call" | custom-call | tf_op jit(solution)/shard_map/pallas_call | solution.py:385
  47.7 1.3 %copy.9 = f32[16,128]{1,0:T(8,128)} copy(f32[16,128]{1,0:T(8,128)} %shard_map.64) | data formatting | bytes 16384

commit v3 on v2

--- a/solution.py
+++ b/solution.py
@@ -70,6 +70,9 @@
             device_id={"store": target}, device_id_type=pl.DeviceIdType.MESH,
         )
 
+    def group_wait(ref, sem):
+        pltpu.make_async_copy(ref, ref, sem).wait()
+
     def each(first, last, body, unroll=1):
         def step(i, carry):
             body(i)
@@ -102,7 +105,7 @@
 
     def list_copy(d):
         return to(
-            my_list.at[0:1], lists_v.at[d, 0:1], list_s.at[d], list_r.at[d], x_peer(d)
+            my_list.at[0:1], lists_v.at[d, 0:1], list_s, list_r, x_peer(d)
         )
 
     each(1, X, lambda d: list_copy(d).start())
@@ -116,7 +119,7 @@
         cut = pl.ds(part * size, size)
         return to(
             src.at[cut], bufs[step].at[cut],
-            ring_s.at[direction, step, part], ring_r.at[direction, step, part],
+            ring_s.at[direction, step], ring_r.at[direction, step, part],
             y_peer(1 if direction == 0 else Y - 1),
         )
 
@@ -142,7 +145,7 @@
 
 
     def block_copy(k, d):
-        return to(stage.at[k, d], table.at[k, d], block_s.at[k, d], block_r.at[k, d], x_peer(d))
+        return to(stage.at[k, d], table.at[k, d], block_s.at[k], block_r.at[k], x_peer(d))
 
     def owner(k, d):
         shift = (0, Y - 1, 1, Y - 2, 2, Y - 3, 3, 4)[k]
@@ -170,7 +173,7 @@
                 tiles[plan_s[0, entry] & 63], kron, preferred_element_type=F32
             )
 
-        each(1, X, lambda d: block_copy(k, d).wait_recv())
+        group_wait(table.at[k, pl.ds(1, X - 1)], block_r.at[k])
         each(0, X, one, unroll=4)
 
     def forward(step):
@@ -249,7 +252,7 @@
 
     gram_part[...] = gram_add(own)
     forward(1)
-    each(1, X, lambda d: list_copy(d).wait_recv())
+    group_wait(lists_v.at[pl.ds(1, X - 1), 0:1], list_r)
     load(lists_v, lists_s, 6).wait()
     serve(0, own)
     serve(1, right1)
@@ -273,18 +276,18 @@
 
     def gram_x_copy(d):
         return to(
-            gram_part.at[pl.ds(y * 16, 16)], gram_x.at[q], gx_s.at[d], gx_r.at[d], x_peer(d)
+            gram_part.at[pl.ds(y * 16, 16)], gram_x.at[q], gx_s, gx_r, x_peer(d)
         )
 
     def gram_g_copy(e):
-        return to(gram_sum, gram.at[y], gg_s.at[e], gg_r.at[e], y_peer(e))
+        return to(gram_sum, gram.at[y], gg_s, gg_r, y_peer(e))
 
     each(1, X, lambda d: gram_x_copy(d).start())
     load_tiles.wait()
     load_plan.wait()
     for k in range(5):
         contribute(k)
-    each(1, X, lambda d: gram_x_copy(d).wait_recv())
+    group_wait(gram_x.at[pl.ds(0, X - 1)], gx_r)
     total = gram_x[0]
     for i in range(1, X):
         total = total + gram_x[i]
@@ -319,14 +322,14 @@
     def rx_copy(d, part):
         return to(
             send_x.at[(q + d) % X, cuts[part]], recv_x.at[d, cuts[part]],
-            rx_s.at[part, d], rx_r.at[part, d], x_peer(d),
+            rx_s.at[part], rx_r.at[part], x_peer(d),
         )
 
     def ry_copy(e):
-        return to(send_y.at[(e + 5) % Y], recv_y.at[e], ry_s.at[e], ry_r.at[e], y_peer(e))
+        return to(send_y.at[(e + 5) % Y], recv_y.at[e], ry_s, ry_r, y_peer(e))
 
     def sum_x(part):
-        each(1, X, lambda d: rx_copy(d, part).wait_recv())
+        group_wait(recv_x.at[pl.ds(1, X - 1), cuts[part]], rx_r.at[part])
         share = send_x[q, cuts[part]].astype(F32)
         for d in range(1, X):
             share = share + recv_x[d, cuts[part]].astype(F32)
@@ -334,7 +337,7 @@
 
     for part in range(2):
         each(1, X, lambda d: rx_copy(d, part).start())
-    each(1, Y, lambda e: gram_g_copy(e).wait_recv())
+    group_wait(gram.at[pl.ds(0, Y - 1)], gg_r)
     gram_day = lax.dot_general(
         day_ref[...], day_ref[...], (((0,), (0,)), ((), ())), preferred_element_type=F32
     )
@@ -349,27 +352,23 @@
     gj_end(lax.fori_loop(10, 16, gj_step, state))
 
     for direction in range(2):
-        for step in range(4):
-            for part in range(parts):
-                if step < 3 or part // 2 == direction:
-                    ring(direction, step, part).wait_send()
+        for step in range(3):
+            group_wait(own, ring_s.at[direction, step])
+        group_wait(own.at[pl.ds(0, SB // 2)], ring_s.at[direction, 3])
     for k in range(8):
-        each(1, X, lambda d: block_copy(k, d).wait_send())
-
-    def sent(d):
-        list_copy(d).wait_send()
-        gram_x_copy(d).wait_send()
-        gram_g_copy(d).wait_send()
-        rx_copy(d, 0).wait_send()
-        rx_copy(d, 1).wait_send()
-
-    each(1, 8, sent)
-
-    each(1, Y, lambda e: ry_copy(e).wait_recv())
+        group_wait(stage.at[k, pl.ds(1, X - 1)], block_s.at[k])
+
+    group_wait(lists_v.at[pl.ds(1, X - 1), 0:1], list_s)
+    group_wait(gram_x.at[pl.ds(0, X - 1)], gx_s)
+    group_wait(gram.at[pl.ds(0, Y - 1)], gg_s)
+    for part in range(2):
+        group_wait(recv_x.at[pl.ds(1, X - 1), cuts[part]], rx_s.at[part])
+
+    group_wait(recv_y.at[pl.ds(1, Y - 1)], ry_r)
     mine = send_y[5].astype(F32)
     for e in range(1, Y):
         mine = mine + recv_y[e].astype(F32)
-    each(1, Y, lambda e: ry_copy(e).wait_send())
+    group_wait(recv_y.at[pl.ds(1, Y - 1)], ry_s)
     out_ref[...] = jnp.dot(mine, inverse[...], precision=HIGHEST, preferred_element_type=F32)
 
 
@@ -410,11 +409,11 @@
             pltpu.VMEM((Y, 16, RANK), bf16),
             pltpu.VMEM((Y, 16, RANK), bf16),
             dma((8,)),
-            dma((2, 4, 4)), dma((2, 4, 4)),
+            dma((2, 4)), dma((2, 4, 4)),
+            dma, dma,
             dma((8,)), dma((8,)),
-            dma((8, 8)), dma((8, 8)),
-            dma((8,)), dma((8,)), dma((8,)), dma((8,)),
-            dma((2, 8)), dma((2, 8)), dma((8,)), dma((8,)),
+            dma, dma, dma, dma,
+            dma((2,)), dma((2,)), dma, dma,
         ],
         compiler_params=pltpu.CompilerParams(
             collective_id=0, has_side_effects=True, vmem_limit_bytes=60 * 1024 * 1024

time: 49.2 us -> 47.2 us (0.959)
  Pallas kernels: 47.1 us -> 45.1 us
    pallas_call x1, Pallas kernels: 47.1 us -> 45.1 us  [local(): pl.pallas_call(kernel, out_shape=jax.ShapeDtypeStruct((16, RANK), F32), i...]
where the time goes in v3:
time: 47.2 us; the launch traced here: 47 us
  Pallas kernels  45.1 us (96%)
  local copies, waits for them, and re-layouts  1.3 us (3%)
  between operations  0.66 us (1%)
    pallas_call x1, Pallas kernels, local(): pl.pallas_call(kernel, out_shape=jax.ShapeDtypeStruct((16, RANK), F32), i...  45.1 us
    unnamed x1, local copies, waits for them, and re-layouts  1.3 us

profile of v3, /device:TPU:1, one launch (start us, length us, event | category | flops | bytes accessed | tf_op | source)
XLA Modules:
  0.0 47.0 jit_solution(15301559007249758828)
XLA Ops:
  0.7 45.1 %shard_map.64 = f32[16,128]{1,0:T(8,128)} custom-call(bf16[64,64,512]{2,1,0:T(8,128)(2,1)} %tiles_hbm.1, s32[2,64]{1,0:T(2,128)} %bitcast.6, s32[1]{0:T(128)S(6)} %copy.8.count_ref, s32[1,64]{1,0:T(1,128)} %bitcast.7, bf16[8,64,128]{2,1,0:T(8,128)(2,1)} %bitcast.5, bf16[8,128]{1,0:T(8,128)(2,1)} %day_hbm.1), custom_call_target="tpu_custom_call" | custom-call | tf_op jit(solution)/shard_map/pallas_call | solution.py:384
  45.7 1.3 %copy.9 = f32[16,128]{1,0:T(8,128)} copy(f32[16,128]{1,0:T(8,128)} %shard_map.64) | data formatting | bytes 16384

commit v4 on v3

--- a/solution.py
+++ b/solution.py
@@ -119,7 +119,7 @@
         cut = pl.ds(part * size, size)
         return to(
             src.at[cut], bufs[step].at[cut],
-            ring_s.at[direction, step], ring_r.at[direction, step, part],
+            ring_s, ring_r.at[direction, step, part],
             y_peer(1 if direction == 0 else Y - 1),
         )
 
@@ -145,7 +145,7 @@
 
 
     def block_copy(k, d):
-        return to(stage.at[k, d], table.at[k, d], block_s.at[k], block_r.at[k], x_peer(d))
+        return to(stage.at[k, d], table.at[k, d], block_s, block_r.at[k], x_peer(d))
 
     def owner(k, d):
         shift = (0, Y - 1, 1, Y - 2, 2, Y - 3, 3, 4)[k]
@@ -305,8 +305,8 @@
 
     lax.fori_loop(0, 64, add, jnp.zeros((TS, RANK), F32), unroll=8)
 
-    def pick(i):
-        place = (i + Y - y + 5) % Y
+    def pick(place):
+        i = (y + place + 3) % Y
         for j in range(2):
             p = 2 * i + j
             end = plan_s[3, p]
@@ -315,7 +315,6 @@
             for part in range(4):
                 send_x[4 * j + part, place] = value[16 * part : 16 * part + 16]
 
-    each(0, 8, pick, unroll=2)
 
     cuts = (pl.ds(0, 3), pl.ds(3, 5))
 
@@ -335,28 +334,26 @@
             share = share + recv_x[d, cuts[part]].astype(F32)
         send_y[cuts[part]] = share.astype(jnp.bfloat16)
 
-    for part in range(2):
-        each(1, X, lambda d: rx_copy(d, part).start())
+    each(0, 3, pick, unroll=3)
+    each(1, X, lambda d: rx_copy(d, 0).start())
+    each(3, 8, pick, unroll=5)
+    each(1, X, lambda d: rx_copy(d, 1).start())
     group_wait(gram.at[pl.ds(0, Y - 1)], gg_r)
     gram_day = lax.dot_general(
         day_ref[...], day_ref[...], (((0,), (0,)), ((), ())), preferred_element_type=F32
     )
     inverse[...] = gram[...].reshape(RANK, RANK) * gram_day
-    state = lax.fori_loop(0, 8, gj_step, gj_start())
+    state = lax.fori_loop(0, 6, gj_step, gj_start())
     sum_x(0)
     each(3, 6, lambda e: ry_copy(e).start())
-    state = lax.fori_loop(8, 10, gj_step, state)
+    state = lax.fori_loop(6, 8, gj_step, state)
     sum_x(1)
     each(1, 3, lambda e: ry_copy(e).start())
     each(6, 8, lambda e: ry_copy(e).start())
-    gj_end(lax.fori_loop(10, 16, gj_step, state))
-
-    for direction in range(2):
-        for step in range(3):
-            group_wait(own, ring_s.at[direction, step])
-        group_wait(own.at[pl.ds(0, SB // 2)], ring_s.at[direction, 3])
-    for k in range(8):
-        group_wait(stage.at[k, pl.ds(1, X - 1)], block_s.at[k])
+    gj_end(lax.fori_loop(8, 16, gj_step, state))
+
+    group_wait(stage.at[pl.ds(0, 8), pl.ds(1, X - 1)], ring_s)
+    group_wait(stage.at[pl.ds(0, 8), pl.ds(1, X - 1)], block_s)
 
     group_wait(lists_v.at[pl.ds(1, X - 1), 0:1], list_s)
     group_wait(gram_x.at[pl.ds(0, X - 1)], gx_s)
@@ -409,9 +406,9 @@
             pltpu.VMEM((Y, 16, RANK), bf16),
             pltpu.VMEM((Y, 16, RANK), bf16),
             dma((8,)),
-            dma((2, 4)), dma((2, 4, 4)),
+            dma, dma((2, 4, 4)),
             dma, dma,
-            dma((8,)), dma((8,)),
+            dma, dma((8,)),
             dma, dma, dma, dma,
             dma((2,)), dma((2,)), dma, dma,
         ],

time: 47.2 us -> 46.6 us (0.987)
  Pallas kernels: 45.1 us -> 44.4 us
    pallas_call x1, Pallas kernels: 45.1 us -> 44.4 us  [local(): pl.pallas_call(kernel, out_shape=jax.ShapeDtypeStruct((16, RANK), F32), i...]
where the time goes in v4:
time: 46.6 us; the launch traced here: 46.4 us
  Pallas kernels  44.4 us (95%)
  local copies, waits for them, and re-layouts  1.3 us (3%)
  between operations  0.66 us (1%)
    pallas_call x1, Pallas kernels, local(): pl.pallas_call(kernel, out_shape=jax.ShapeDtypeStruct((16, RANK), F32), i...  44.4 us
    unnamed x1, local copies, waits for them, and re-layouts  1.3 us

profile of v4, /device:TPU:1, one launch (start us, length us, event | category | flops | bytes accessed | tf_op | source)
XLA Modules:
  0.0 46.4 jit_solution(12838913232175564145)
XLA Ops:
  0.7 44.4 %shard_map.64 = f32[16,128]{1,0:T(8,128)} custom-call(bf16[64,64,512]{2,1,0:T(8,128)(2,1)} %tiles_hbm.1, s32[2,64]{1,0:T(2,128)} %bitcast.6, s32[1]{0:T(128)S(6)} %copy.8.count_ref, s32[1,64]{1,0:T(1,128)} %bitcast.7, bf16[8,64,128]{2,1,0:T(8,128)(2,1)} %bitcast.5, bf16[8,128]{1,0:T(8,128)(2,1)} %day_hbm.1), custom_call_target="tpu_custom_call" | custom-call | tf_op jit(solution)/shard_map/pallas_call | solution.py:381
  45.1 1.3 %copy.9 = f32[16,128]{1,0:T(8,128)} copy(f32[16,128]{1,0:T(8,128)} %shard_map.64) | data formatting | bytes 16384

commit v5 on v4

--- a/solution.py
+++ b/solution.py
@@ -176,8 +176,8 @@
         group_wait(table.at[k, pl.ds(1, X - 1)], block_r.at[k])
         each(0, X, one, unroll=4)
 
-    def forward(step):
-        for part in range(parts):
+    def forward(step, first=0, last=parts):
+        for part in range(first, last):
             for direction in range(2):
                 ring(direction, step - 1, part).wait_recv()
                 if step < 3 or part // 2 == direction:
@@ -251,9 +251,11 @@
         gj_apply(state[1], state[2], RANK - 8)
 
     gram_part[...] = gram_add(own)
-    forward(1)
+    forward(1, 0, 2)
     group_wait(lists_v.at[pl.ds(1, X - 1), 0:1], list_r)
-    load(lists_v, lists_s, 6).wait()
+    load_lists = load(lists_v, lists_s, 6)
+    forward(1, 2)
+    load_lists.wait()
     serve(0, own)
     serve(1, right1)
     serve(2, left1)

time: 46.6 us -> 46.5 us (level)
  no operation moved by 1% of the time
where the time goes in v5:
time: 46.5 us; the launch traced here: 46.3 us
  Pallas kernels  44.4 us (95%)
  local copies, waits for them, and re-layouts  1.3 us (3%)
  between operations  0.66 us (1%)
    pallas_call x1, Pallas kernels, local(): pl.pallas_call(kernel, out_shape=jax.ShapeDtypeStruct((16, RANK), F32), i...  44.4 us
    unnamed x1, local copies, waits for them, and re-layouts  1.3 us

profile of v5, /device:TPU:1, one launch (start us, length us, event | category | flops | bytes accessed | tf_op | source)
XLA Modules:
  0.0 46.3 jit_solution(13779377598191495548)
XLA Ops:
  0.7 44.4 %shard_map.64 = f32[16,128]{1,0:T(8,128)} custom-call(bf16[64,64,512]{2,1,0:T(8,128)(2,1)} %tiles_hbm.1, s32[2,64]{1,0:T(2,128)} %bitcast.6, s32[1]{0:T(128)S(6)} %copy.8.count_ref, s32[1,64]{1,0:T(1,128)} %bitcast.7, bf16[8,64,128]{2,1,0:T(8,128)(2,1)} %bitcast.5, bf16[8,128]{1,0:T(8,128)(2,1)} %day_hbm.1), custom_call_target="tpu_custom_call" | custom-call | tf_op jit(solution)/shard_map/pallas_call | solution.py:383
  45.0 1.3 %copy.9 = f32[16,128]{1,0:T(8,128)} copy(f32[16,128]{1,0:T(8,128)} %shard_map.64) | data formatting | bytes 16384
